TPU v7x, 32 devices: a whole 2x2x4 slice. The times are simulated.
32 devices in a mesh: groups: 2 (over x), mem: 16 (over z, y, core).
Axes of the slice: x: 2, y: 2, z: 4, core: 2. Of those that a mesh axis runs over, the one named last changes fastest.
Arguments:
- hidden: bfloat16 [16384, 2560], P(('groups', 'mem')), parts along dimension 0, may hold values from -6 to 6
- cotangent: bfloat16 [16384, 2560], P(('groups', 'mem')), parts along dimension 0, may hold values from -6 to 6
- hash_ids: int32 [16384, 4], P(('groups', 'mem')), parts along dimension 0, may hold values from 0 to 16383, as said below
- seq_lengths: int32 [32, 4], P(('groups', 'mem')), parts along dimension 0, may hold values from 1 to 256, 512 in all within a row
- hash_table: bfloat16 [16384, 128], P('mem'), may hold values from -6 to 6
- w_key: bfloat16 [512, 2560], replicated, may hold values from -0.25 to 0.25
- w_value: bfloat16 [512, 2560], replicated, may hold values from -0.25 to 0.25
- conv_weight: float32 [4, 2560], replicated, may hold values from -3 to 3
Outputs:
- new_hidden: bfloat16 [16384, 2560], P(('groups', 'mem')), parts along dimension 0
- grad_hidden: bfloat16 [16384, 2560], P(('groups', 'mem')), parts along dimension 0
- table_grad: float32 [32768, 128], P(('groups', 'mem')), parts along dimension 0
There are 2 independent parts, one for each index of `groups`. A program takes and returns all parts, laid end to end along the dimension named above; an argument that names none is the same for every part. Nothing has to cross between parts.
Inputs may be any that keep to these rules, and one draw needn't show every extreme that they name: `hash_ids`: row r lies in table block r // 1024. Among the 2048 ids of one device's tokens at most 256 lie in any one block; one block receives exactly 256 from every device's tokens.
All inputs are finite; a program needn't handle non-finite values.
Results may differ from a plain program's by a relative error of at most 0.0028.
Values may be sent and summed in bfloat16 or wider, within the bound.
A program may use at most 128 MiB of HBM per device.

v0:
```python
import math

import jax
import jax.numpy as jnp
from jax import lax
from jax.sharding import PartitionSpec as P

epsilon = 1e-06


def rms_scaled(vectors):
    return vectors * lax.rsqrt(jnp.mean(vectors * vectors, axis=-1, keepdims=True) + epsilon)


def positions(seq_lengths, block_len):
    seq_ends = jnp.cumsum(seq_lengths, axis=1)
    steps_in = jnp.arange(block_len, dtype=jnp.int32)
    before = (seq_ends[:, None, :] <= steps_in[None, :, None]).astype(jnp.int32)
    starts = jnp.sum(before * seq_lengths[:, None, :], axis=2)
    return (steps_in[None, :] - starts).reshape(-1)


def layer_part(hidden32, key_proj, value_proj, conv_weight, within):
    columns = hidden32.shape[1]
    scores = jnp.sum(
        rms_scaled(hidden32) * rms_scaled(key_proj), axis=1, keepdims=True
    ) / math.sqrt(columns)
    carried = jax.nn.sigmoid(scores) * value_proj
    convolved = jnp.zeros_like(carried)
    for offset in range(conv_weight.shape[0]):
        delayed = jnp.pad(carried, ((offset, 0), (0, 0)))[: carried.shape[0]]
        convolved = convolved + conv_weight[offset] * jnp.where(
            (within >= offset)[:, None], delayed, 0.0
        )
    return hidden32 + carried + jax.nn.silu(convolved)


def back_project(grads, weight):
    return lax.dot_general(
        grads, weight, (((1,), (1,)), ((), ())), preferred_element_type=jnp.float32
    )


def local(hidden, cotangent, hash_ids, seq_lengths, hash_table, w_key, w_value, conv_weight):
    shards = lax.axis_size("mem")
    rows_held = hash_table.shape[0]
    row_width = hash_table.shape[1]
    wanted = hash_ids.reshape(-1)
    capacity = 2 * wanted.shape[0] // shards
    owners = wanted // rows_held
    offsets = wanted - owners * rows_held
    belongs = (owners[:, None] == jnp.arange(shards, dtype=jnp.int32)[None, :]).astype(jnp.int32)
    earlier = jnp.cumsum(belongs, axis=0) - belongs
    places = jnp.sum(earlier * belongs, axis=1)
    slot_at = owners * capacity + places
    requests = (
        jnp.full((shards * capacity,), -1, jnp.int32)
        .at[slot_at]
        .set(offsets)
        .reshape(shards, capacity)
    )
    asked_rows = lax.all_to_all(requests, "mem", split_axis=0, concat_axis=0, tiled=True)
    replies, asked_rows = (
        lax.all_to_all(
            jnp.take(hash_table, jnp.maximum(asked_rows, 0), axis=0),
            "mem",
            split_axis=0,
            concat_axis=0,
            tiled=True,
        ),
        asked_rows,
    )
    fetched = replies.reshape(-1, row_width)[slot_at].reshape(hidden.shape[0], -1)
    key_proj = jnp.dot(fetched, w_key, preferred_element_type=jnp.float32)
    value_proj = jnp.dot(fetched, w_value, preferred_element_type=jnp.float32)
    within = positions(seq_lengths, hidden.shape[0])

    def forward(hidden32, keys_in, values_in):
        return layer_part(hidden32, keys_in, values_in, conv_weight, within)

    output, pullback = jax.vjp(forward, hidden.astype(jnp.float32), key_proj, value_proj)
    d_hidden, d_key, d_value = pullback(cotangent.astype(jnp.float32))
    d_fetched = back_project(d_key.astype(jnp.bfloat16), w_key) + back_project(
        d_value.astype(jnp.bfloat16), w_value
    )
    outgoing = (
        jnp.zeros((shards * capacity, row_width), jnp.float32)
        .at[slot_at]
        .set(d_fetched.reshape(-1, row_width))
    )
    outgoing = outgoing.reshape(shards, capacity, row_width)
    targets = jnp.where(asked_rows >= 0, asked_rows, rows_held).reshape(-1)
    incoming = lax.all_to_all(outgoing, "mem", split_axis=0, concat_axis=0, tiled=True)
    flat = incoming.reshape(-1, incoming.shape[2])
    table_grad = (
        jnp.zeros((rows_held, incoming.shape[2]), jnp.float32).at[targets].add(flat, mode="drop")
    )
    return (output.astype(jnp.bfloat16), d_hidden.astype(jnp.bfloat16), table_grad)


def solution(mesh):
    return jax.shard_map(
        local,
        mesh=mesh,
        in_specs=(
            P(("groups", "mem"), None),
            P(("groups", "mem"), None),
            P(("groups", "mem"), None),
            P(("groups", "mem"), None),
            P("mem", None),
            P(),
            P(),
            P(),
        ),
        out_specs=(
            P(("groups", "mem"), None),
            P(("groups", "mem"), None),
            P(("groups", "mem"), None),
        ),
        check_vma=False,
    )
```

profile of v0, /device:TPU:15, one launch (start us, length us, event | category | flops | bytes accessed | tf_op | source)
XLA Modules:
  0.0 220.1 jit_solution(3544724736385622188)
XLA Ops:
  0.6 0.0 copy-start
  0.7 1.0 copy.21
  1.7 0.2 reshape.362
  1.8 0.2 reshape.361
  2.0 0.2 reshape.360
  2.2 4.5 %reduce-window.6 = s32[16,16,128]{2,1,0:T(8,128)S(1)} reduce-window(s32[16,16,128]{2,1,0:T(8,128)S(1)} %fusion.38, s32[]{:T(128)} %constant.80.clone.1), window={size=1x1x128 pad=0_0x0_0x127_0}, to_apply=%region_1.2 | reduce-window | flops 4161536 | bytes 262148 | tf_op jit(solution)/shard_map/reduce-window
  6.8 0.4 slice_reduce_fusion
  7.2 0.2 reduce-window.9
  7.4 0.1 broadcast_add_fusion
  7.5 0.1 fusion.37
  7.6 0.1 compare_select_fusion.2
  7.6 8.1 %scatter_custom_fusion = s32[4096]{0:T(1024)S(1)} fusion(s32[2048]{0:T(1024)S(1)} %bitcast.52, s32[2048]{0:T(1024)S(1)} %get-tuple-element.16, s32[]{:T(128)} %constant.78.clone.1), kind=kCustom, calls=%fused_computation.105 | custom fusion | bytes 16388 | tf_op jit(solution)/shard_map/scatter | solution.py:59
  15.7 10.5 %all_to_all.22 = s32[16,1,256]{2,1,0:T(1,128)S(1)} all-to-all(s32[16,1,256]{2,1,0:T(1,128)S(1)} %bitcast.49), channel_id=1, replica_groups=mesh['groups'=2,'mem'=16] {'mem'}, dimensions={0} | all-to-all | bytes 32768 | tf_op jit(solution)/shard_map/all_to_all | solution.py:62
  26.2 0.0 copy-start.8
  26.2 0.0 copy-start.7
  26.2 15.0 %gather_fusion = bf16[4096,128]{1,0:T(8,128)(2,1)} fusion(bf16[1024,128]{1,0:T(8,128)(2,1)S(1)} %copy-done.1, s32[4096]{0:T(1024)S(1)} %broadcast_clamp_fusion), kind=kCustom, calls=%fused_computation | custom fusion | bytes 2113536 | tf_op jit(solution)/shard_map/jit(_take)/gather | solution.py:65
  41.3 2.5 %broadcast_select_fusion = bf16[16,256,128]{2,1,0:T(8,128)(2,1)} fusion(bf16[16,256,128]{2,1,0:T(8,128)(2,1)} %bitcast.46, pred[16,256]{1,0:T(8,128)(4,1)S(1)} %compare_bitcast_fusion), kind=kLoop, calls=%fused_computation.63 | loop fusion | flops 524288 | bytes 2101248 | tf_op jit(solution)/shard_map/jit(_take)/select_n | solution.py:65
  43.8 6.6 %all-to-all-start.1 = ((bf16[16,256,128]{2,1,0:T(8,128)(2,1)}), bf16[16,256,128]{2,1,0:T(8,128)(2,1)}, u32[]{:S(2)}, u32[]{:S(2)}) async-start(bf16[16,256,128]{2,1,0:T(8,128)(2,1)} %broadcast_select_fusion), calls=%async_computation.1 | async-start | bytes 2097152 | tf_op jit(solution)/shard_map/all_to_all | solution.py:64
  50.4 0.0 copy-done.8
  50.4 0.2 reduce_window_sum.28
  50.6 0.1 select_reduce_fusion
  50.7 0.1 slice_reduce_fusion.4
  50.8 2.3 %fusion.22 = f32[512]{0:T(512)S(1)} fusion(bf16[512,2560]{1,0:T(8,128)(2,1)} %param.8), kind=kLoop, calls=%fused_computation.45 | loop fusion | flops 3931648 | bytes 2623488 | tf_op jit(solution)/shard_map/jvp()/reduce_sum | solution.py:12
  53.1 22.3 %all-to-all-done.1 = bf16[16,256,128]{2,1,0:T(8,128)(2,1)} async-done(((bf16[16,256,128]{2,1,0:T(8,128)(2,1)}), bf16[16,256,128]{2,1,0:T(8,128)(2,1)}, u32[]{:S(2)}, u32[]{:S(2)}) %all-to-all-start.1) | async-done | bytes 1048608 | tf_op jit(solution)/shard_map/all_to_all | solution.py:64
  75.4 9.1 %gather_fusion.1 = bf16[2048,128]{1,0:T(8,128)(2,1)} fusion(bf16[4096,128]{1,0:T(8,128)(2,1)} %bitcast.6, s32[2048]{0:T(1024)S(1)} %broadcast_clamp_fusion.1), kind=kCustom, calls=%fused_computation.1 | custom fusion | bytes 1056768 | tf_op jit(solution)/shard_map/gather | solution.py:73
  84.4 1.4 reshape.365
  85.8 0.0 copy-start.3
  85.8 3.5 %multiply_reduce_fusion.1 = (f32[512]{0:T(512)S(1)}, f32[512,2560]{1,0:T(8,128)S(1)}) fusion(bf16[512,512]{1,0:T(8,128)(2,1)S(1)} %reshape.365, bf16[512,2560]{1,0:T(8,128)(2,1)} %param.13), kind=kOutput, calls=%fused_computation.55 | convolution fusion | flops 1344798208 | bytes 8390656 | tf_op jit(solution)/shard_map/dot_general | solution.py:74
  89.3 0.0 copy-done.3
  89.4 1.0 fusion.17
  90.4 0.0 copy-start.5
  90.4 3.9 %broadcast_multiply_fusion = (f32[512,2560]{1,0:T(8,128)S(1)}, f32[512,2560]{1,0:T(8,128)}) fusion(f32[512]{0:T(512)S(1)} %add_divide_fusion.1, bf16[512,512]{1,0:T(8,128)(2,1)S(1)} %reshape.365, bf16[512,2560]{1,0:T(8,128)(2,1)S(1)} %copy-done), kind=kOutput, calls=%fused_computation.58 | convolution fusion | flops 1343488000 | bytes 13633536 | tf_op jit(solution)/shard_map/dot_general | solution.py:75
  94.3 0.0 copy-done.5
  94.3 8.7 %multiply_select_fusion.2 = (f32[512,2560]{1,0:T(8,128)}, f32[512,2560]{1,0:T(8,128)}) fusion(f32[2560]{0:T(1024)S(1)} %get-tuple-element.7, pred[512]{0:T(512)(128)(4,1)S(1)} %get-tuple-element.21, bf16[512,2560]{1,0:T(8,128)(2,1)S(1)} %copy-done.5, f32[512,2560]{1,0:T(8,128)S(1)} %get-tuple-element.24, pred[512]{0:T(512)(128)(4,1)S(1)} %get-tuple-element.20, ...), kind=kLoop, calls=%fused_computation.53 | loop fusion | flops 30146560 | bytes 18393088 | tf_op jit(solution)/shard_map/transpose(jvp(jit(_where)))/select_n | solution.py:32
  103.0 0.0 copy-done.4
  103.0 7.4 %multiply_select_fusion.1 = (f32[512,2560]{1,0:T(8,128)}, f32[512,2560]{1,0:T(8,128)}) fusion(f32[2560]{0:T(1024)S(1)} %get-tuple-element.8, pred[512]{0:T(512)(128)(4,1)S(1)} %get-tuple-element.20, f32[512,2560]{1,0:T(8,128)} %get-tuple-element.12, bf16[512,2560]{1,0:T(8,128)(2,1)S(1)} %copy-done.5, f32[2560]{0:T(1024)S(1)} %get-tuple-element.6, ...), kind=kLoop, calls=%fused_computation.52 | loop fusion | flops 18350080 | bytes 18371584 | tf_op jit(solution)/shard_map/transpose(jvp(jit(_where)))/select_n | solution.py:32
  110.4 16.5 %multiply_reduce_fusion = (f32[512]{0:T(512)S(1)}, f32[512,2560]{1,0:T(8,128)}, bf16[512,2560]{1,0:T(8,128)(2,1)}) fusion(f32[512,2560]{1,0:T(8,128)} %get-tuple-element.25, f32[512,2560]{1,0:T(8,128)} %get-tuple-element.12, f32[2560]{0:T(1024)S(1)} %get-tuple-element.5, pred[512]{0:T(512)(128)(4,1)S(1)} %get-tuple-element.18, ...), kind=kLoop, calls=%fused_computation.50 | loop fusion | flops 30146048 | bytes 44577280 | tf_op jit(solution)/shard_map/transpose(jvp())/reduce_sum | solution.py:28
  126.9 0.0 slice-start
  126.9 3.0 %fusion.16 = (f32[512]{0:T(512)S(1)}, f32[512]{0:T(512)S(1)}) fusion(f32[512,2560]{1,0:T(8,128)S(1)} %get-tuple-element.23, bf16[512,2560]{1,0:T(8,128)(2,1)S(1)} %copy-done.3, f32[512]{0:T(512)S(1)} %fusion.47, f32[512]{0:T(512)S(1)} %get-tuple-element.26, f32[512]{0:T(512)S(1)} %get-tuple-element.27), kind=kLoop, calls=%fused_computation.39 | loop fusion | flops 11795456 | bytes 7874560 | tf_op jit(solution)/shard_map/transpose(jvp())/reduce_sum | solution.py:12
  130.0 0.0 slice-start.1
  130.0 2.0 fusion.28
  132.0 2.5 %fusion.30 = f32[512,512]{1,0:T(8,128)} fusion(f32[512,512]{1,0:T(8,128)S(1)} %fusion.28, bf16[512,2560]{1,0:T(8,128)(2,1)S(1)} %copy-done, f32[512,2560]{1,0:T(8,128)S(1)} %bitcast.45, f32[512]{0:T(512)S(1)} %add_divide_fusion.1), kind=kOutput, calls=%fused_computation.60 | convolution fusion | flops 1345060864 | bytes 9963520 | tf_op jit(solution)/shard_map/dot_general | solution.py:39
  134.5 2.3 %reshape.397 = f32[2048,128]{1,0:T(8,128)} reshape(f32[512,512]{1,0:T(8,128)} %fusion.30) | data formatting | bytes 2097152 | tf_op jit(solution)/shard_map/reshape | solution.py:89
  136.8 7.4 %scatter_custom_fusion.1 = f32[4096,128]{1,0:T(8,128)} fusion(s32[2048]{0:T(1024)S(1)} %bitcast.54, f32[2048,128]{1,0:T(8,128)} %reshape.397, f32[]{:T(128)} %constant.75.clone.1), kind=kCustom, calls=%fused_computation.61 | custom fusion | bytes 2097664 | tf_op jit(solution)/shard_map/scatter | solution.py:89
  144.2 4.9 %all-to-all-start.2 = ((f32[16,256,128]{2,1,0:T(8,128)}), f32[16,256,128]{2,1,0:T(8,128)}, u32[]{:S(2)}, u32[]{:S(2)}) async-start(f32[16,256,128]{2,1,0:T(8,128)} %bitcast.43), calls=%async_computation.2 | async-start | bytes 4194304 | tf_op jit(solution)/shard_map/all_to_all | solution.py:93
  149.2 6.3 %fusion.20 = bf16[512,2560]{1,0:T(8,128)(2,1)} fusion(bf16[512,2560]{1,0:T(8,128)(2,1)} %param.9, bf16[512,2560]{1,0:T(8,128)(2,1)} %param.8, f32[512,2560]{1,0:T(8,128)} %copy-done.2, f32[512]{0:T(512)S(1)} %multiply_multiply_fusion.1, f32[512]{0:T(512)S(1)} %fusion.47, f32[512]{0:T(512)S(1)} %get-tuple-element.27, f32[512]{0:T(512)S(1)} %get-tuple-element.26), kind=kLoop, calls=%fused_computation.43 | loop fusion | flops 13107200 | bytes 13115392 | tf_op jit(solution)/shard_map/convert_element_type | solution.py:98
  155.4 41.2 %all-to-all-done.2 = f32[16,256,128]{2,1,0:T(8,128)} async-done(((f32[16,256,128]{2,1,0:T(8,128)}), f32[16,256,128]{2,1,0:T(8,128)}, u32[]{:S(2)}, u32[]{:S(2)}) %all-to-all-start.2) | async-done | bytes 2097184 | tf_op jit(solution)/shard_map/all_to_all | solution.py:93
  196.6 23.4 %scatter_custom_fusion.2 = f32[1024,128]{1,0:T(8,128)} fusion(s32[4096]{0:T(1024)S(1)} %bitcast.56, f32[4096,128]{1,0:T(8,128)} %bitcast.12, f32[]{:T(128)} %constant.75.clone.1), kind=kCustom, calls=%fused_computation.64 | custom fusion | flops 524288 | bytes 524800 | tf_op jit(solution)/shard_map/scatter-add | solution.py:96
  (27 shorter events, 0.2 us)
Async XLA Ops:
  0.6 89.7 %copy-start = (bf16[512,2560]{1,0:T(8,128)(2,1)S(1)}, bf16[512,2560]{1,0:T(8,128)(2,1)}, u32[]{:S(2)}) copy-start(bf16[512,2560]{1,0:T(8,128)(2,1)} %param.14) | copy-start | bytes 7864324
  0.6 25.5 %copy-start.1 = (bf16[1024,128]{1,0:T(8,128)(2,1)S(1)}, bf16[1024,128]{1,0:T(8,128)(2,1)}, u32[]{:S(2)}) copy-start(bf16[1024,128]{1,0:T(8,128)(2,1)} %param.12) | copy-start | bytes 786436
  26.2 24.2 %copy-start.8 = (s32[1,4]{1,0:T(1,128)S(1)}, s32[1,4]{1,0:T(1,128)}, u32[]{:S(2)}) copy-start(s32[1,4]{1,0:T(1,128)} %param.11) | copy-start | bytes 52
  26.2 24.5 %copy-start.7 = (f32[4,2560]{1,0:T(4,128)S(1)}, f32[4,2560]{1,0:T(4,128)}, u32[]{:S(2)}) copy-start(f32[4,2560]{1,0:T(4,128)} %param.15) | copy-start | bytes 122884
  43.8 31.6 %all-to-all-start.1 = ((bf16[16,256,128]{2,1,0:T(8,128)(2,1)}), bf16[16,256,128]{2,1,0:T(8,128)(2,1)}, u32[]{:S(2)}, u32[]{:S(2)}) async-start(bf16[16,256,128]{2,1,0:T(8,128)(2,1)} %broadcast_select_fusion), calls=%async_computation.1 | async-start | bytes 2097152 | tf_op jit(solution)/shard_map/all_to_all | solution.py:64
  85.8 3.5 %copy-start.3 = (bf16[512,2560]{1,0:T(8,128)(2,1)S(1)}, bf16[512,2560]{1,0:T(8,128)(2,1)}, u32[]{:S(2)}) copy-start(bf16[512,2560]{1,0:T(8,128)(2,1)} %param.8) | copy-start | bytes 7864324
  89.3 40.6 %copy-start.2 = (f32[512,2560]{1,0:T(8,128)}, f32[512,2560]{1,0:T(8,128)S(1)}, u32[]{:S(2)}) copy-start(f32[512,2560]{1,0:T(8,128)S(1)} %get-tuple-element.23) | copy-start | bytes 15728644
  90.4 3.9 %copy-start.5 = (bf16[512,2560]{1,0:T(8,128)(2,1)S(1)}, bf16[512,2560]{1,0:T(8,128)(2,1)}, u32[]{:S(2)}) copy-start(bf16[512,2560]{1,0:T(8,128)(2,1)} %param.9) | copy-start | bytes 7864324
  94.3 8.7 %copy-start.4 = (f32[512,2560]{1,0:T(8,128)}, f32[512,2560]{1,0:T(8,128)S(1)}, u32[]{:S(2)}) copy-start(f32[512,2560]{1,0:T(8,128)S(1)} %get-tuple-element.24) | copy-start | bytes 15728644
  126.9 3.0 %copy-start.6 = (bf16[512,2560]{1,0:T(8,128)(2,1)S(1)}, bf16[512,2560]{1,0:T(8,128)(2,1)}, u32[]{:S(2)}) copy-start(bf16[512,2560]{1,0:T(8,128)(2,1)} %param.13) | copy-start | bytes 7864324
  126.9 5.0 %slice-start = ((s8[5242880]{0:T(1024)(128)(4,1)}), s8[4194304]{0:T(1024)(128)(4,1)S(1)}, s32[]{:S(2)}) async-start(s8[5242880]{0:T(1024)(128)(4,1)} %bitcast.44), calls=%async_computation.3 | async-start | bytes 8388608
  130.0 2.0 slice-start.1
  144.2 52.4 %all-to-all-start.2 = ((f32[16,256,128]{2,1,0:T(8,128)}), f32[16,256,128]{2,1,0:T(8,128)}, u32[]{:S(2)}, u32[]{:S(2)}) async-start(f32[16,256,128]{2,1,0:T(8,128)} %bitcast.43), calls=%async_computation.2 | async-start | bytes 4194304 | tf_op jit(solution)/shard_map/all_to_all | solution.py:93
where the time goes:
time: 221 us; the launch traced here: 220 us
  other arithmetic  76.5 us (35%)
  waiting for transfers between devices  63.5 us (29%)
  local copies, waits for them, and re-layouts  45.3 us (20%)
  matrix products  11.9 us (5%)
  starting transfers between devices  11.5 us (5%)
  blocking collectives  10.5 us (5%)
    all_to_all x1, waiting for transfers between devices, local(): lax.all_to_all(outgoing, 'mem', split_axis=0, concat_axis=0, tiled=True)  41.2 us
    scatter-add x1, other arithmetic, local(): jnp.zeros((rows_held, incoming.shape[2]), jnp.float32).at[targets]  23.4 us
    all_to_all x1, waiting for transfers between devices, local(): lax.all_to_all(jnp.take(hash_table, jnp.maximum(asked_rows, 0), axis=0),...  22.3 us
    reduce_sum x1, other arithmetic, layer_part(): carried = jax.nn.sigmoid(scores) * value_proj  16.5 us
    select_n x2, other arithmetic, layer_part(): jnp.where((within >= offset)[:, None], delayed, 0.0)  16.1 us
    gather x1, local copies, waits for them, and re-layouts, local(): jnp.take(hash_table, jnp.maximum(asked_rows, 0), axis=0)  15 us
    all_to_all x1, blocking collectives, local(): lax.all_to_all(requests, 'mem', split_axis=0, concat_axis=0, tiled=True)  10.5 us
    gather x1, local copies, waits for them, and re-layouts, local(): replies.reshape(-1, row_width)[slot_at].reshape(hidden.shape[0], -1)  9.07 us
  transfers between devices with their start and end apart: 2, of which 2 were waited for; matrix products, arithmetic and copies ran while one was open for 4% of the time, Pallas kernels for 0%

commit v1 on v0

v1 whole, which is shorter than its diff:
```python
import functools
import math

import jax
import jax.numpy as jnp
from jax import lax
from jax.experimental import pallas as pl
from jax.experimental.pallas import tpu as pltpu
from jax.sharding import PartitionSpec as P

epsilon = 1e-06
LANES = 128
bf16 = jnp.bfloat16
f32 = jnp.float32
i32 = jnp.int32
NT = (((1,), (1,)), ((), ()))


def dot(a, b, dims=(((1,), (0,)), ((), ()))):
    return lax.dot_general(a, b, dims, preferred_element_type=f32)


def iota(shape, dim):
    return lax.broadcasted_iota(i32, shape, dim)


def one_hot(match):
    return jnp.where(match, 1.0, 0.0).astype(bf16)


def partner(me, step, shards):
    total, bit = 0, 1
    while bit < shards:
        total = total + (((me // bit) % 2 + (step // bit) % 2) % 2) * bit
        bit *= 2
    return total


def greet(me, shards):
    barrier = pltpu.get_barrier_semaphore()

    def tell(step, carry):
        pl.semaphore_signal(barrier, inc=1, device_id={"mem": partner(me, step, shards)})
        return carry

    lax.fori_loop(1, shards, tell, 0)
    pl.semaphore_wait(barrier, shards - 1)


def as_column(row):
    return jnp.transpose(jnp.broadcast_to(row, (LANES, row.shape[1])))


def fetch_kernel(shards, cap, ids_ref, table_ref, fetched_ref, slots_ref, asked_ref,
                 requests, answers, replies, columns, total,
                 ask_send, ask_recv, row_send, row_recv):
    me = lax.axis_index("mem")
    heads, tokens = ids_ref.shape
    rows = table_ref.shape[0]
    wide = requests.shape[2]

    def ask(peer):
        return pltpu.make_async_remote_copy(
            src_ref=requests.at[peer], dst_ref=asked_ref.at[me],
            send_sem=ask_send.at[peer], recv_sem=ask_recv.at[me], device_id={"mem": peer})

    def asked_by(peer):
        return pltpu.make_async_remote_copy(
            src_ref=requests.at[peer], dst_ref=asked_ref.at[peer],
            send_sem=ask_send.at[peer], recv_sem=ask_recv.at[peer], device_id={"mem": peer})

    def reply(peer):
        return pltpu.make_async_remote_copy(
            src_ref=answers.at[peer], dst_ref=replies.at[me],
            send_sem=row_send.at[peer], recv_sem=row_recv.at[me], device_id={"mem": peer})

    def reply_of(peer):
        return pltpu.make_async_remote_copy(
            src_ref=answers.at[peer], dst_ref=replies.at[peer],
            send_sem=row_send.at[peer], recv_sem=row_recv.at[peer], device_id={"mem": peer})

    earlier = one_hot(iota((tokens, tokens), 0) < iota((tokens, tokens), 1))
    seen = jnp.zeros((shards, 1), f32)
    gathered = jnp.zeros((3 * shards, wide), f32)
    for h in range(heads):
        ids = ids_ref[h:h + 1, :]
        owner = ids // rows
        offset = ids - owner * rows
        mine = jnp.where(jnp.broadcast_to(owner, (shards, tokens)) == iota((shards, tokens), 0), 1.0, 0.0)
        ranks = dot(mine.astype(bf16), earlier) + seen
        seen = seen + jnp.sum(mine, axis=1, keepdims=True)
        rank = jnp.sum(mine * ranks, axis=0, keepdims=True).astype(i32)
        slot = owner * cap + rank
        slots_ref[h:h + 1, :] = slot
        columns[h] = as_column(slot)
        at_rank = one_hot(jnp.broadcast_to(rank, (wide, tokens)) == iota((wide, tokens), 0))
        high = (offset // 256).astype(f32)
        low = (offset % 256).astype(f32)
        parts = jnp.concatenate([mine * high, mine * low, mine], axis=0).astype(bf16)
        gathered = gathered + dot(parts, at_rank, NT)
    wanted = gathered[:shards] * 256.0 + gathered[shards:2 * shards]
    wanted = jnp.where(gathered[2 * shards:] > 0.5, wanted, -1.0).astype(i32)
    for peer in range(shards):
        requests[peer] = wanted[peer:peer + 1, :]

    greet(me, shards)

    def ask_all(j, carry):
        ask(partner(me, shards - j, shards)).start()
        return carry

    lax.fori_loop(1, shards, ask_all, 0)
    asked_ref[me] = requests[me]

    def rows_for(peer):
        column = as_column(asked_ref[peer])[:cap]
        hot = jnp.concatenate(
            [one_hot(column == iota((cap, LANES), 1) + start) for start in range(0, rows, LANES)], axis=1)
        return dot(hot, table_ref[...]).astype(bf16)

    def answer(j, carry):
        peer = partner(me, shards - j, shards)
        asked_by(peer).wait_recv()
        answers[peer] = rows_for(peer)
        reply(peer).start()
        return carry

    lax.fori_loop(1, shards, answer, 0)
    replies[me] = rows_for(me)

    def unpack(peer):
        block = replies[peer]
        for h in range(heads):
            base = peer * cap
            column = columns[h] - base
            if cap % LANES == 0:
                hot = jnp.concatenate(
                    [one_hot(column == iota((tokens, LANES), 1) + start) for start in range(0, cap, LANES)], axis=1)
            else:
                hot = one_hot(column == iota((tokens, LANES), 1))[:, :cap]
            total[:, h * LANES:(h + 1) * LANES] += dot(hot, block)

    total[...] = jnp.zeros_like(total)
    unpack(me)

    def take(step, carry):
        peer = partner(me, step, shards)
        reply_of(peer).wait_recv()
        unpack(peer)
        return carry

    lax.fori_loop(1, shards, take, 0)
    fetched_ref[...] = total[...].astype(bf16)

    def finish(step, carry):
        peer = partner(me, step, shards)
        ask(peer).wait_send()
        reply(peer).wait_send()
        return carry

    lax.fori_loop(1, shards, finish, 0)


def fetch(ids, table, shards, cap):
    heads, tokens = ids.shape
    width = table.shape[1]
    wide = max(cap, LANES)
    vmem = pl.BlockSpec(memory_space=pltpu.VMEM)
    return pl.pallas_call(
        functools.partial(fetch_kernel, shards, cap),
        out_shape=(
            jax.ShapeDtypeStruct((tokens, heads * width), bf16),
            jax.ShapeDtypeStruct((heads, tokens), i32),
            jax.ShapeDtypeStruct((shards, 1, wide), i32),
        ),
        in_specs=[vmem, vmem],
        out_specs=(vmem, vmem, vmem),
        scratch_shapes=[
            pltpu.VMEM((shards, 1, wide), i32),
            pltpu.VMEM((shards, cap, width), bf16),
            pltpu.VMEM((shards, cap, width), bf16),
            pltpu.VMEM((heads, tokens, LANES), i32),
            pltpu.VMEM((tokens, heads * width), f32),
            pltpu.SemaphoreType.DMA((shards,)),
            pltpu.SemaphoreType.DMA((shards,)),
            pltpu.SemaphoreType.DMA((shards,)),
            pltpu.SemaphoreType.DMA((shards,)),
        ],
        compiler_params=pltpu.CompilerParams(
            collective_id=0, has_side_effects=True, vmem_limit_bytes=24 * 2**20),
        name="fetch",
    )(ids, table)


def layer_kernel(lengths_ref, fetched_ref, hidden_ref, cotangent_ref, wk_ref, wv_ref, conv_ref,
                 out_ref, grad_ref, pieces_ref,
                 keys, values, dvalues, dkeys, masks, ahead, carried, dconv,
                 sums, gates, dgate, total):
    tokens, columns = hidden_ref.shape
    taps = conv_ref.shape[0]
    shape = (tokens, LANES)
    block = 512 if columns % 512 == 0 else LANES
    chunk = 128

    def within(position):
        start = jnp.zeros(shape, i32)
        end = 0
        for s in range(lengths_ref.shape[1]):
            length = lengths_ref[0, s]
            end = end + length
            start = start + jnp.where(position >= end, length, 0)
        return position - start

    here = iota(shape, 0)
    for k in range(1, taps):
        masks[k - 1] = jnp.where(within(here) >= k, 1.0, 0.0)
        ahead[k - 1] = jnp.where((within(here + k) >= k) & (here + k < tokens), 1.0, 0.0)
    sums[...] = jnp.zeros_like(sums)
    dgate[...] = jnp.zeros_like(dgate)
    carried[0:8] = jnp.zeros((8, LANES), f32)
    dconv[tokens:tokens + 8] = jnp.zeros((8, LANES), f32)

    def project(j, carry):
        at = pl.ds(pl.multiple_of(j * block, block), block)
        key = dot(fetched_ref[...], wk_ref[:, at])
        keys[:, at] = key
        values[:, at] = dot(fetched_ref[...], wv_ref[:, at])
        for c in range(0, block, LANES):
            hid = hidden_ref[:, pl.ds(pl.multiple_of(j * block + c, LANES), LANES)].astype(f32)
            part = key[:, c:c + LANES]
            sums[0] += part * part
            sums[1] += part * hid
            sums[2] += hid * hid
        return carry

    lax.fori_loop(0, columns // block, project, 0)
    inv = 1.0 / columns
    k_scale = lax.rsqrt(jnp.sum(sums[0], axis=1, keepdims=True) * inv + epsilon)
    h_scale = lax.rsqrt(jnp.sum(sums[2], axis=1, keepdims=True) * inv + epsilon)
    cross = jnp.sum(sums[1], axis=1, keepdims=True)
    score = cross * k_scale * h_scale * (1.0 / math.sqrt(columns))
    gate = 0.5 + 0.5 * jnp.tanh(0.5 * score)
    gates[...] = jnp.broadcast_to(gate, shape)

    def mix(j, carry):
        at = pl.ds(pl.multiple_of(j * LANES, LANES), LANES)
        w = [conv_ref[k:k + 1, at] for k in range(taps)]
        for r in range(0, tokens, chunk):
            carried[8 + r:8 + r + chunk] = gates[r:r + chunk] * values[r:r + chunk, at]
        for r in range(0, tokens, chunk):
            now = carried[8 + r:8 + r + chunk]
            conv = w[0] * now
            for k in range(1, taps):
                conv = conv + w[k] * (masks[k - 1, r:r + chunk] * carried[8 + r - k:8 + r - k + chunk])
            sig = 0.5 + 0.5 * jnp.tanh(0.5 * conv)
            silu = conv * sig
            out_ref[r:r + chunk, at] = (hidden_ref[r:r + chunk, at].astype(f32) + now + silu).astype(bf16)
            dconv[r:r + chunk] = cotangent_ref[r:r + chunk, at].astype(f32) * (sig + silu * (1.0 - sig))
        for r in range(0, tokens, chunk):
            dcarried = cotangent_ref[r:r + chunk, at].astype(f32) + w[0] * dconv[r:r + chunk]
            for k in range(1, taps):
                dcarried = dcarried + w[k] * (ahead[k - 1, r:r + chunk] * dconv[r + k:r + k + chunk])
            dvalues[r:r + chunk, at] = (gates[r:r + chunk] * dcarried).astype(bf16)
            dgate[r:r + chunk] += values[r:r + chunk, at] * dcarried
        return carry

    lax.fori_loop(0, columns // LANES, mix, 0)
    dscore = jnp.sum(dgate[...], axis=1, keepdims=True) * gate * (1.0 - gate) * (1.0 / math.sqrt(columns))
    both = dscore * k_scale * h_scale
    sums[0] = jnp.broadcast_to(both, shape)
    sums[1] = jnp.broadcast_to(both * h_scale * h_scale * cross * inv, shape)
    sums[2] = jnp.broadcast_to(both * k_scale * k_scale * cross * inv, shape)
    total[...] = jnp.zeros_like(total)

    def back(j, carry):
        at = pl.ds(pl.multiple_of(j * block, block), block)
        for c in range(0, block, LANES):
            col = pl.ds(pl.multiple_of(j * block + c, LANES), LANES)
            for r in range(0, tokens, chunk):
                row = slice(r, r + chunk)
                hid = hidden_ref[row, col].astype(f32)
                key = keys[row, col]
                a = sums[0, row]
                grad_ref[row, col] = (
                    cotangent_ref[row, col].astype(f32) + (a * key - sums[1, row] * hid)).astype(bf16)
                dkeys[row, c:c + LANES] = (a * hid - sums[2, row] * key).astype(bf16)
        total[...] += dot(dkeys[...], wk_ref[:, at], NT) + dot(dvalues[:, at], wv_ref[:, at], NT)
        return carry

    lax.fori_loop(0, columns // block, back, 0)
    pieces_ref[...] = total[...].astype(bf16)


def layer(lengths, fetched, hidden, cotangent, w_key, w_value, conv_weight):
    tokens, columns = hidden.shape
    depth = fetched.shape[1]
    taps = conv_weight.shape[0]
    vmem = pl.BlockSpec(memory_space=pltpu.VMEM)
    block = 512 if columns % 512 == 0 else LANES
    return pl.pallas_call(
        layer_kernel,
        out_shape=(
            jax.ShapeDtypeStruct((tokens, columns), bf16),
            jax.ShapeDtypeStruct((tokens, columns), bf16),
            jax.ShapeDtypeStruct((tokens, depth), bf16),
        ),
        in_specs=[pl.BlockSpec(memory_space=pltpu.SMEM)] + [vmem] * 6,
        out_specs=(vmem, vmem, vmem),
        scratch_shapes=[
            pltpu.VMEM((tokens, columns), f32),
            pltpu.VMEM((tokens, columns), f32),
            pltpu.VMEM((tokens, columns), bf16),
            pltpu.VMEM((tokens, block), bf16),
            pltpu.VMEM((taps - 1, tokens, LANES), f32),
            pltpu.VMEM((taps - 1, tokens, LANES), f32),
            pltpu.VMEM((tokens + 8, LANES), f32),
            pltpu.VMEM((tokens + 8, LANES), f32),
            pltpu.VMEM((3, tokens, LANES), f32),
            pltpu.VMEM((tokens, LANES), f32),
            pltpu.VMEM((tokens, LANES), f32),
            pltpu.VMEM((tokens, depth), f32),
        ],
        compiler_params=pltpu.CompilerParams(vmem_limit_bytes=48 * 2**20),
        name="layer",
    )(lengths, fetched, hidden, cotangent, w_key, w_value, conv_weight)


def spread_kernel(shards, cap, slots_ref, asked_ref, pieces_ref, grad_ref, outgoing, incoming, send, recv):
    me = lax.axis_index("mem")
    heads, tokens = slots_ref.shape
    rows = grad_ref.shape[0]

    def push(peer):
        return pltpu.make_async_remote_copy(
            src_ref=outgoing.at[peer], dst_ref=incoming.at[me],
            send_sem=send.at[peer], recv_sem=recv.at[me], device_id={"mem": peer})

    def pushed_by(peer):
        return pltpu.make_async_remote_copy(
            src_ref=outgoing.at[peer], dst_ref=incoming.at[peer],
            send_sem=send.at[peer], recv_sem=recv.at[peer], device_id={"mem": peer})

    def pack(peer):
        packed = jnp.zeros((cap, LANES), f32)
        for h in range(heads):
            row = slots_ref[h:h + 1, :] - peer * cap
            hot = one_hot(jnp.broadcast_to(row, (cap, tokens)) == iota((cap, tokens), 0))
            packed = packed + dot(hot, pieces_ref[:, h * LANES:(h + 1) * LANES])
        return packed.astype(bf16)

    greet(me, shards)

    def send_one(j, carry):
        peer = partner(me, shards - j, shards)
        outgoing[peer] = pack(peer)
        push(peer).start()
        return carry

    lax.fori_loop(1, shards, send_one, 0)
    incoming[me] = pack(me)

    def add(peer):
        row = asked_ref[peer][:, :cap]
        hot = one_hot(jnp.broadcast_to(row, (rows, cap)) == iota((rows, cap), 0))
        return dot(hot, incoming[peer])

    grad_ref[...] = add(me)

    def take(step, carry):
        peer = partner(me, step, shards)
        pushed_by(peer).wait_recv()
        grad_ref[...] += add(peer)
        return carry

    lax.fori_loop(1, shards, take, 0)

    def finish(step, carry):
        push(partner(me, step, shards)).wait_send()
        return carry

    lax.fori_loop(1, shards, finish, 0)


def spread(slots, asked, pieces, rows, shards, cap):
    vmem = pl.BlockSpec(memory_space=pltpu.VMEM)
    return pl.pallas_call(
        functools.partial(spread_kernel, shards, cap),
        out_shape=jax.ShapeDtypeStruct((rows, LANES), f32),
        in_specs=[vmem] * 3,
        out_specs=vmem,
        scratch_shapes=[
            pltpu.VMEM((shards, cap, LANES), bf16),
            pltpu.VMEM((shards, cap, LANES), bf16),
            pltpu.SemaphoreType.DMA((shards,)),
            pltpu.SemaphoreType.DMA((shards,)),
        ],
        compiler_params=pltpu.CompilerParams(
            collective_id=1, has_side_effects=True, vmem_limit_bytes=24 * 2**20),
        name="spread",
    )(slots, asked, pieces)


def local(hidden, cotangent, hash_ids, seq_lengths, hash_table, w_key, w_value, conv_weight):
    shards = lax.axis_size("mem")
    cap = 2 * hash_ids.size // shards
    fetched, slots, asked = fetch(hash_ids.T, hash_table, shards, cap)
    new_hidden, grad_hidden, pieces = layer(
        seq_lengths, fetched, hidden, cotangent, w_key, w_value, conv_weight)
    table_grad = spread(slots, asked, pieces, hash_table.shape[0], shards, cap)
    return new_hidden, grad_hidden, table_grad


def solution(mesh):
    tokens = P(("groups", "mem"), None)
    return jax.shard_map(
        local,
        mesh=mesh,
        in_specs=(tokens, tokens, tokens, tokens, P("mem", None), P(), P(), P()),
        out_specs=(tokens, tokens, tokens),
        check_vma=False,
    )
```

time: 221 us -> 101 us (0.46)
  the two profiles are of different devices: /device:TPU:15 before, /device:TPU:0 now
where the time goes in v1:
time: 101 us
  Pallas kernels  94.7 us (94%)
  local copies, waits for them, and re-layouts  5.6 us (6%)
    pallas_call x1, Pallas kernels, fetch(): pl.pallas_call(functools.partial(fetch_kernel, shards, cap), out_shape=(j...  39.5 us
    pallas_call x1, Pallas kernels, spread(): pl.pallas_call(functools.partial(spread_kernel, shards, cap), out_shape=j...  31.3 us
    pallas_call x1, Pallas kernels, layer(): pl.pallas_call(layer_kernel, out_shape=(jax.ShapeDtypeStruct((tokens, col...  23.9 us
    unnamed x11, local copies, waits for them, and re-layouts  5.6 us

profile of v1, /device:TPU:0, one launch (start us, length us, event | category | flops | bytes accessed | tf_op | source)
XLA Modules:
  0.0 101.0 jit_solution(3974316493527691890)
XLA Ops:
  0.6 0.0 copy-start.1
  0.6 0.9 copy-done.1
  1.6 0.0 copy-start.3
  1.6 0.7 copy-done.3
  2.3 39.5 %fetch.1 = (bf16[512,512]{1,0:T(8,128)(2,1)S(1)}, s32[4,512]{1,0:T(4,128)S(1)}, s32[16,1,256]{2,1,0:T(1,128)S(1)}) custom-call(s32[4,512]{1,0:T(4,128)S(1)} %bitcast.1, bf16[1024,128]{1,0:T(8,128)(2,1)S(1)} %copy-done.1), custom_call_target="tpu_custom_call" | custom-call | tf_op jit(solution)/shard_map/fetch/pallas_call | solution.py:169
  41.8 0.0 copy-start
  41.8 1.7 %copy-done = bf16[512,2560]{1,0:T(8,128)(2,1)S(1)} copy-done((bf16[512,2560]{1,0:T(8,128)(2,1)S(1)}, bf16[512,2560]{1,0:T(8,128)(2,1)}, u32[]{:S(2)}) %copy-start) | copy-done | bytes 2621464
  43.5 0.0 copy-start.2
  43.5 0.8 copy-done.2
  44.3 0.0 copy-start.4
  44.3 0.7 copy-done.4
  44.9 23.9 %layer.1 = (bf16[512,2560]{1,0:T(8,128)(2,1)}, bf16[512,2560]{1,0:T(8,128)(2,1)}, bf16[512,512]{1,0:T(8,128)(2,1)S(1)}) custom-call(s32[1,4]{1,0:T(1,128)S(1)} %copy-done.4, bf16[512,512]{1,0:T(8,128)(2,1)S(1)} %get-tuple-element.9.fetched_ref, bf16[512,2560]{1,0:T(8,128)(2,1)S(1)} %copy-done, bf16[512,2560]{1,0:T(8,128)(2,1)} %cotangent_ref.1, ...), custom_call_target="tpu_custom_call" | custom-call | tf_op jit(solution)/shard_map/layer/pallas_call | solution.py:300
  68.8 31.3 %spread.1 = f32[1024,128]{1,0:T(8,128)S(1)} custom-call(s32[4,512]{1,0:T(4,128)S(1)} %get-tuple-element.12.slots_ref, s32[16,1,256]{2,1,0:T(1,128)S(1)} %get-tuple-element.13.asked_ref, bf16[512,512]{1,0:T(8,128)(2,1)S(1)} %get-tuple-element.14.pieces_ref), custom_call_target="tpu_custom_call" | custom-call | tf_op jit(solution)/shard_map/spread/pallas_call | solution.py:386
  100.2 0.8 copy.12
Async XLA Ops:
  0.6 1.0 copy-start.1
  1.6 0.7 copy-start.3
  41.8 1.7 %copy-start = (bf16[512,2560]{1,0:T(8,128)(2,1)S(1)}, bf16[512,2560]{1,0:T(8,128)(2,1)}, u32[]{:S(2)}) copy-start(bf16[512,2560]{1,0:T(8,128)(2,1)} %hidden_ref.1) | copy-start | bytes 7864324
  43.5 0.8 copy-start.2
  44.3 0.7 copy-start.4

commit v2 on v1

--- a/solution.py
+++ b/solution.py
@@ -10,6 +10,8 @@
 
 epsilon = 1e-06
 LANES = 128
+LAYER_VMEM = 60 * 2**20
+SWAP_VMEM = 60 * 2**20
 bf16 = jnp.bfloat16
 f32 = jnp.float32
 i32 = jnp.int32
@@ -36,48 +38,58 @@
     return total
 
 
-def greet(me, shards):
+def greet(peers):
     barrier = pltpu.get_barrier_semaphore()
-
-    def tell(step, carry):
-        pl.semaphore_signal(barrier, inc=1, device_id={"mem": partner(me, step, shards)})
-        return carry
-
-    lax.fori_loop(1, shards, tell, 0)
-    pl.semaphore_wait(barrier, shards - 1)
+    for peer in peers:
+        pl.semaphore_signal(barrier, inc=1, device_id=peer)
+    pl.semaphore_wait(barrier, len(peers))
 
 
 def as_column(row):
     return jnp.transpose(jnp.broadcast_to(row, (LANES, row.shape[1])))
 
 
-def fetch_kernel(shards, cap, ids_ref, table_ref, fetched_ref, slots_ref, asked_ref,
-                 requests, answers, replies, columns, total,
-                 ask_send, ask_recv, row_send, row_recv):
-    me = lax.axis_index("mem")
+def fetch_kernel(shards, cap, ids_hbm, table_hbm, fetched_ref, slots_ref, asked_ref,
+                 table, mirror, requests, asks, answers, replies, columns, total,
+                 ask_send, ask_recv, row_send, row_recv, far_send, far_recv, swap_send, swap_recv,
+                 tell_send, tell_recv, table_sem, ids_ref, ids_sem):
+    me, group = lax.axis_index("mem"), lax.axis_index("groups")
+    groups = lax.axis_size("groups")
+    half = shards // 2
+    home = me // half
+    opposite = partner(me, half, shards)
     heads, tokens = ids_ref.shape
-    rows = table_ref.shape[0]
-    wide = requests.shape[2]
-
-    def ask(peer):
+    rows = table.shape[0]
+    wide = requests.shape[3]
+    far = {"mem": opposite}
+    twin = {"groups": partner(group, 1, 2) + (group // 2) * 2}
+    share = rows // 2 if groups % 2 == 0 else rows
+    mine_at = pl.ds(pl.multiple_of((group % 2) * share, 16), share) if share < rows else pl.ds(0, rows)
+    twin_at = pl.ds(pl.multiple_of((1 - group % 2) * share, 16), share)
+
+    def remote(src, dst, send, recv, device):
         return pltpu.make_async_remote_copy(
-            src_ref=requests.at[peer], dst_ref=asked_ref.at[me],
-            send_sem=ask_send.at[peer], recv_sem=ask_recv.at[me], device_id={"mem": peer})
-
-    def asked_by(peer):
-        return pltpu.make_async_remote_copy(
-            src_ref=requests.at[peer], dst_ref=asked_ref.at[peer],
-            send_sem=ask_send.at[peer], recv_sem=ask_recv.at[peer], device_id={"mem": peer})
-
-    def reply(peer):
-        return pltpu.make_async_remote_copy(
-            src_ref=answers.at[peer], dst_ref=replies.at[me],
-            send_sem=row_send.at[peer], recv_sem=row_recv.at[me], device_id={"mem": peer})
-
-    def reply_of(peer):
-        return pltpu.make_async_remote_copy(
-            src_ref=answers.at[peer], dst_ref=replies.at[peer],
-            send_sem=row_send.at[peer], recv_sem=row_recv.at[peer], device_id={"mem": peer})
+            src_ref=src, dst_ref=dst, send_sem=send, recv_sem=recv, device_id=device)
+
+    def ask(peer, slot):
+        at = peer % half
+        return remote(requests.at[:, at], asks.at[:, slot], ask_send.at[at], ask_recv.at[slot], {"mem": peer})
+
+    def reply(peer, side, slot):
+        at = peer % half
+        return remote(answers.at[side, at], replies.at[side, slot],
+                      row_send.at[side, at], row_recv.at[side, slot], {"mem": peer})
+
+    here = me % half
+    ids_load = pltpu.make_async_copy(ids_hbm, ids_ref, ids_sem)
+    ids_load.start()
+    greet([{"mem": partner(me, step, shards)} for step in range(1, half)] + [far]
+          + ([twin] if share < rows else []))
+    to_far = remote(table_hbm.at[mine_at], mirror.at[mine_at], far_send, far_recv, far)
+    to_far.start()
+    table_load = pltpu.make_async_copy(table_hbm, table, table_sem)
+    table_load.start()
+    ids_load.wait()
 
     earlier = one_hot(iota((tokens, tokens), 0) < iota((tokens, tokens), 1))
     seen = jnp.zeros((shards, 1), f32)
@@ -100,38 +112,45 @@
         gathered = gathered + dot(parts, at_rank, NT)
     wanted = gathered[:shards] * 256.0 + gathered[shards:2 * shards]
     wanted = jnp.where(gathered[2 * shards:] > 0.5, wanted, -1.0).astype(i32)
-    for peer in range(shards):
-        requests[peer] = wanted[peer:peer + 1, :]
-
-    greet(me, shards)
+    for block in range(shards):
+        requests[(block // half + home) % 2, block % half] = wanted[block:block + 1, :]
 
     def ask_all(j, carry):
-        ask(partner(me, shards - j, shards)).start()
-        return carry
-
-    lax.fori_loop(1, shards, ask_all, 0)
-    asked_ref[me] = requests[me]
-
-    def rows_for(peer):
-        column = as_column(asked_ref[peer])[:cap]
+        ask(partner(me, half - j, shards), here).start()
+        return carry
+
+    lax.fori_loop(1, half, ask_all, 0)
+    asks[:, here] = requests[:, here]
+    table_load.wait()
+
+    def rows_for(side, peer, held):
+        column = as_column(asks[side, peer % half])[:cap]
         hot = jnp.concatenate(
             [one_hot(column == iota((cap, LANES), 1) + start) for start in range(0, rows, LANES)], axis=1)
-        return dot(hot, table_ref[...]).astype(bf16)
+        return dot(hot, held[...]).astype(bf16)
 
     def answer(j, carry):
-        peer = partner(me, shards - j, shards)
-        asked_by(peer).wait_recv()
-        answers[peer] = rows_for(peer)
-        reply(peer).start()
-        return carry
-
-    lax.fori_loop(1, shards, answer, 0)
-    replies[me] = rows_for(me)
-
-    def unpack(peer):
-        block = replies[peer]
+        peer = partner(me, half - j, shards)
+        ask(peer, peer % half).wait_recv()
+        answers[0, peer % half] = rows_for(0, peer, table)
+        reply(peer, 0, here).start()
+        return carry
+
+    lax.fori_loop(1, half, answer, 0)
+    asked_ref[0] = asks[0]
+    tell = remote(asks.at[1], asked_ref.at[1], tell_send, tell_recv, far)
+    tell.start()
+
+    to_far.wait_recv()
+    if share < rows:
+        swap = remote(mirror.at[mine_at], mirror.at[mine_at], swap_send, swap_recv, twin)
+        swap.start()
+    replies[0, here] = rows_for(0, me, table)
+
+    def unpack(side, peer):
+        block = replies[side, peer % half]
+        base = ((home + side) % 2 * half + peer % half) * cap
         for h in range(heads):
-            base = peer * cap
             column = columns[h] - base
             if cap % LANES == 0:
                 hot = jnp.concatenate(
@@ -141,66 +160,104 @@
             total[:, h * LANES:(h + 1) * LANES] += dot(hot, block)
 
     total[...] = jnp.zeros_like(total)
-    unpack(me)
-
-    def take(step, carry):
-        peer = partner(me, step, shards)
-        reply_of(peer).wait_recv()
-        unpack(peer)
-        return carry
-
-    lax.fori_loop(1, shards, take, 0)
+    unpack(0, me)
+    if share < rows:
+        remote(mirror.at[twin_at], mirror.at[twin_at], swap_send, swap_recv, twin).wait_recv()
+
+    def answer_far(j, carry):
+        peer = partner(me, half - j, shards)
+        answers[1, peer % half] = rows_for(1, peer, mirror)
+        reply(peer, 1, here).start()
+        return carry
+
+    lax.fori_loop(1, half, answer_far, 0)
+    replies[1, here] = rows_for(1, me, mirror)
+    unpack(1, me)
+
+    for side in range(2):
+        def take(step, carry):
+            peer = partner(me, step, shards)
+            reply(peer, side, peer % half).wait_recv()
+            unpack(side, peer)
+            return carry
+
+        lax.fori_loop(1, half, take, 0)
     fetched_ref[...] = total[...].astype(bf16)
 
     def finish(step, carry):
         peer = partner(me, step, shards)
-        ask(peer).wait_send()
-        reply(peer).wait_send()
-        return carry
-
-    lax.fori_loop(1, shards, finish, 0)
+        ask(peer, here).wait_send()
+        reply(peer, 0, here).wait_send()
+        reply(peer, 1, here).wait_send()
+        return carry
+
+    lax.fori_loop(1, half, finish, 0)
+    to_far.wait_send()
+    if share < rows:
+        swap.wait_send()
+    tell.wait()
 
 
 def fetch(ids, table, shards, cap):
     heads, tokens = ids.shape
-    width = table.shape[1]
+    rows, width = table.shape
     wide = max(cap, LANES)
+    half = shards // 2
     vmem = pl.BlockSpec(memory_space=pltpu.VMEM)
+    anywhere = pl.BlockSpec(memory_space=pltpu.HBM)
+    dma = pltpu.SemaphoreType.DMA
     return pl.pallas_call(
         functools.partial(fetch_kernel, shards, cap),
         out_shape=(
             jax.ShapeDtypeStruct((tokens, heads * width), bf16),
             jax.ShapeDtypeStruct((heads, tokens), i32),
-            jax.ShapeDtypeStruct((shards, 1, wide), i32),
+            jax.ShapeDtypeStruct((2, half, 1, wide), i32),
         ),
-        in_specs=[vmem, vmem],
+        in_specs=[anywhere] * 2,
         out_specs=(vmem, vmem, vmem),
         scratch_shapes=[
-            pltpu.VMEM((shards, 1, wide), i32),
-            pltpu.VMEM((shards, cap, width), bf16),
-            pltpu.VMEM((shards, cap, width), bf16),
+            pltpu.VMEM((rows, width), bf16),
+            pltpu.VMEM((rows, width), bf16),
+            pltpu.VMEM((2, half, 1, wide), i32),
+            pltpu.VMEM((2, half, 1, wide), i32),
+            pltpu.VMEM((2, half, cap, width), bf16),
+            pltpu.VMEM((2, half, cap, width), bf16),
             pltpu.VMEM((heads, tokens, LANES), i32),
             pltpu.VMEM((tokens, heads * width), f32),
-            pltpu.SemaphoreType.DMA((shards,)),
-            pltpu.SemaphoreType.DMA((shards,)),
-            pltpu.SemaphoreType.DMA((shards,)),
-            pltpu.SemaphoreType.DMA((shards,)),
+            dma((half,)), dma((half,)), dma((2, half)), dma((2, half)),
+            dma, dma, dma, dma, dma, dma,
+            dma, pltpu.VMEM((heads, tokens), i32), dma,
         ],
         compiler_params=pltpu.CompilerParams(
-            collective_id=0, has_side_effects=True, vmem_limit_bytes=24 * 2**20),
+            collective_id=0, has_side_effects=True, vmem_limit_bytes=SWAP_VMEM),
         name="fetch",
     )(ids, table)
 
 
-def layer_kernel(lengths_ref, fetched_ref, hidden_ref, cotangent_ref, wk_ref, wv_ref, conv_ref,
-                 out_ref, grad_ref, pieces_ref,
-                 keys, values, dvalues, dkeys, masks, ahead, carried, dconv,
+def layer_kernel(lengths_ref, fetched_ref, hidden_hbm, cotangent_hbm, wk_hbm, wv_hbm, conv_hbm,
+                 out_hbm, grad_hbm, pieces_ref,
+                 hidden_ref, cotangent_ref, wk_ref, wv_ref, conv_ref, load_sem, conv_sem,
+                 out_ref, grad_ref, out_sem, grad_sem, keys, values, dvalues, dkeys, masks, ahead, carried, dconv,
                  sums, gates, dgate, total):
     tokens, columns = hidden_ref.shape
     taps = conv_ref.shape[0]
     shape = (tokens, LANES)
     block = 512 if columns % 512 == 0 else LANES
     chunk = 128
+
+    def load(which, j):
+        src, dst = ((wk_hbm, wk_ref), (wv_hbm, wv_ref), (hidden_hbm, hidden_ref),
+                    (cotangent_hbm, cotangent_ref))[which]
+        at = pl.ds(pl.multiple_of(j * block, block), block)
+        return pltpu.make_async_copy(src.at[:, at], dst.at[:, at], load_sem.at[which, j])
+
+    for j in range(columns // block):
+        for which in range(3):
+            load(which, j).start()
+    conv_load = pltpu.make_async_copy(conv_hbm, conv_ref, conv_sem)
+    conv_load.start()
+    for j in range(columns // block):
+        load(3, j).start()
 
     def within(position):
         start = jnp.zeros(shape, i32)
@@ -222,6 +279,8 @@
 
     def project(j, carry):
         at = pl.ds(pl.multiple_of(j * block, block), block)
+        for which in range(3):
+            load(which, j).wait()
         key = dot(fetched_ref[...], wk_ref[:, at])
         keys[:, at] = key
         values[:, at] = dot(fetched_ref[...], wv_ref[:, at])
@@ -241,6 +300,10 @@
     score = cross * k_scale * h_scale * (1.0 / math.sqrt(columns))
     gate = 0.5 + 0.5 * jnp.tanh(0.5 * score)
     gates[...] = jnp.broadcast_to(gate, shape)
+
+    def write(src, dst, sems, j):
+        at = pl.ds(pl.multiple_of(j * block, block), block)
+        return pltpu.make_async_copy(src.at[:, at], dst.at[:, at], sems.at[j])
 
     def mix(j, carry):
         at = pl.ds(pl.multiple_of(j * LANES, LANES), LANES)
@@ -264,7 +327,15 @@
             dgate[r:r + chunk] += values[r:r + chunk, at] * dcarried
         return carry
 
-    lax.fori_loop(0, columns // LANES, mix, 0)
+    conv_load.wait()
+
+    def mix_block(j, carry):
+        load(3, j).wait()
+        lax.fori_loop(j * (block // LANES), (j + 1) * (block // LANES), mix, 0)
+        write(out_ref, out_hbm, out_sem, j).start()
+        return carry
+
+    lax.fori_loop(0, columns // block, mix_block, 0)
     dscore = jnp.sum(dgate[...], axis=1, keepdims=True) * gate * (1.0 - gate) * (1.0 / math.sqrt(columns))
     both = dscore * k_scale * h_scale
     sums[0] = jnp.broadcast_to(both, shape)
@@ -284,11 +355,19 @@
                 grad_ref[row, col] = (
                     cotangent_ref[row, col].astype(f32) + (a * key - sums[1, row] * hid)).astype(bf16)
                 dkeys[row, c:c + LANES] = (a * hid - sums[2, row] * key).astype(bf16)
+        write(grad_ref, grad_hbm, grad_sem, j).start()
         total[...] += dot(dkeys[...], wk_ref[:, at], NT) + dot(dvalues[:, at], wv_ref[:, at], NT)
         return carry
 
     lax.fori_loop(0, columns // block, back, 0)
     pieces_ref[...] = total[...].astype(bf16)
+
+    def finish(j, carry):
+        write(out_ref, out_hbm, out_sem, j).wait()
+        write(grad_ref, grad_hbm, grad_sem, j).wait()
+        return carry
+
+    lax.fori_loop(0, columns // block, finish, 0)
 
 
 def layer(lengths, fetched, hidden, cotangent, w_key, w_value, conv_weight):
@@ -304,9 +383,20 @@
             jax.ShapeDtypeStruct((tokens, columns), bf16),
             jax.ShapeDtypeStruct((tokens, depth), bf16),
         ),
-        in_specs=[pl.BlockSpec(memory_space=pltpu.SMEM)] + [vmem] * 6,
-        out_specs=(vmem, vmem, vmem),
+        in_specs=[pl.BlockSpec(memory_space=pltpu.SMEM), vmem] + [pl.BlockSpec(memory_space=pltpu.HBM)] * 5,
+        out_specs=(pl.BlockSpec(memory_space=pl.ANY), pl.BlockSpec(memory_space=pl.ANY), vmem),
         scratch_shapes=[
+            pltpu.VMEM((tokens, columns), bf16),
+            pltpu.VMEM((tokens, columns), bf16),
+            pltpu.VMEM((depth, columns), bf16),
+            pltpu.VMEM((depth, columns), bf16),
+            pltpu.VMEM((taps, columns), f32),
+            pltpu.SemaphoreType.DMA((4, columns // block)),
+            pltpu.SemaphoreType.DMA,
+            pltpu.VMEM((tokens, columns), bf16),
+            pltpu.VMEM((tokens, columns), bf16),
+            pltpu.SemaphoreType.DMA((columns // block,)),
+            pltpu.SemaphoreType.DMA((columns // block,)),
             pltpu.VMEM((tokens, columns), f32),
             pltpu.VMEM((tokens, columns), f32),
             pltpu.VMEM((tokens, columns), bf16),
@@ -320,7 +410,7 @@
             pltpu.VMEM((tokens, LANES), f32),
             pltpu.VMEM((tokens, depth), f32),
         ],
-        compiler_params=pltpu.CompilerParams(vmem_limit_bytes=48 * 2**20),
+        compiler_params=pltpu.CompilerParams(vmem_limit_bytes=LAYER_VMEM),
         name="layer",
     )(lengths, fetched, hidden, cotangent, w_key, w_value, conv_weight)
 
@@ -348,7 +438,7 @@
             packed = packed + dot(hot, pieces_ref[:, h * LANES:(h + 1) * LANES])
         return packed.astype(bf16)
 
-    greet(me, shards)
+    greet([{"mem": partner(me, step, shards)} for step in range(1, shards)])
 
     def send_one(j, carry):
         peer = partner(me, shards - j, shards)
@@ -360,7 +450,8 @@
     incoming[me] = pack(me)
 
     def add(peer):
-        row = asked_ref[peer][:, :cap]
+        half = shards // 2
+        row = asked_ref[(peer // half + me // half) % 2, peer % half][:, :cap]
         hot = one_hot(jnp.broadcast_to(row, (rows, cap)) == iota((rows, cap), 0))
         return dot(hot, incoming[peer])
 
@@ -395,7 +486,7 @@
             pltpu.SemaphoreType.DMA((shards,)),
         ],
         compiler_params=pltpu.CompilerParams(
-            collective_id=1, has_side_effects=True, vmem_limit_bytes=24 * 2**20),
+            collective_id=1, has_side_effects=True, vmem_limit_bytes=SWAP_VMEM),
         name="spread",
     )(slots, asked, pieces)
 

time: 101 us -> 88.9 us (0.88)
  Pallas kernels: 94.7 us -> 86.2 us
  local copies, waits for them, and re-layouts: 5.6 us -> 1.87 us
    pallas_call x1, Pallas kernels: 39.5 us -> 30.9 us  [fetch(): pl.pallas_call(functools.partial(fetch_kernel, shards, cap), out_shape=(j...]
    unnamed x11 -> x1, local copies, waits for them, and re-layouts: 5.6 us -> 1.87 us
    pallas_call x1, Pallas kernels: 31.3 us -> 32.6 us  [spread(): pl.pallas_call(functools.partial(spread_kernel, shards, cap), out_shape=j...]
    pallas_call x1, Pallas kernels: 23.9 us -> 22.6 us  [layer(): pl.pallas_call(layer_kernel, out_shape=(jax.ShapeDtypeStruct((tokens, col...]
where the time goes in v2:
time: 88.9 us; the launch traced here: 88.7 us
  Pallas kernels  86.2 us (97%)
  local copies, waits for them, and re-layouts  1.87 us (2%)
    pallas_call x1, Pallas kernels, spread(): pl.pallas_call(functools.partial(spread_kernel, shards, cap), out_shape=j...  32.6 us
    pallas_call x1, Pallas kernels, fetch(): pl.pallas_call(functools.partial(fetch_kernel, shards, cap), out_shape=(j...  30.9 us
    pallas_call x1, Pallas kernels, layer(): pl.pallas_call(layer_kernel, out_shape=(jax.ShapeDtypeStruct((tokens, col...  22.6 us
    unnamed x1, local copies, waits for them, and re-layouts  1.87 us

profile of v2, /device:TPU:0, one launch (start us, length us, event | category | flops | bytes accessed | tf_op | source)
XLA Modules:
  0.0 88.7 jit_solution(7662764381645199837)
XLA Ops:
  0.6 30.9 %fetch.1 = (bf16[512,512]{1,0:T(8,128)(2,1)}, s32[4,512]{1,0:T(4,128)}, s32[2,8,1,256]{3,2,1,0:T(1,128)}) custom-call(s32[4,512]{1,0:T(4,128)} %bitcast.1, bf16[1024,128]{1,0:T(8,128)(2,1)} %table_hbm.1), custom_call_target="tpu_custom_call" | custom-call | tf_op jit(solution)/shard_map/fetch/pallas_call | solution.py:209
  31.5 22.6 %layer.1 = (bf16[512,2560]{1,0:T(8,128)(2,1)}, bf16[512,2560]{1,0:T(8,128)(2,1)}, bf16[512,512]{1,0:T(8,128)(2,1)}) custom-call(s32[1,4]{1,0:T(1,128)} %lengths_ref.1, bf16[512,512]{1,0:T(8,128)(2,1)} %get-tuple-element.9.fetched_ref, bf16[512,2560]{1,0:T(8,128)(2,1)} %hidden_hbm.1, bf16[512,2560]{1,0:T(8,128)(2,1)} %cotangent_hbm.1, ...), custom_call_target="tpu_custom_call" | custom-call | tf_op jit(solution)/shard_map/layer/pallas_call | solution.py:379
  54.2 32.6 %spread.1 = f32[1024,128]{1,0:T(8,128)} custom-call(s32[4,512]{1,0:T(4,128)} %get-tuple-element.12.slots_ref, s32[2,8,1,256]{3,2,1,0:T(1,128)} %get-tuple-element.13.asked_ref, bf16[512,512]{1,0:T(8,128)(2,1)} %get-tuple-element.14.pieces_ref), custom_call_target="tpu_custom_call" | custom-call | tf_op jit(solution)/shard_map/spread/pallas_call | solution.py:477
  86.8 1.9 %copy.12 = f32[1024,128]{1,0:T(8,128)} copy(f32[1024,128]{1,0:T(8,128)} %spread.1) | data formatting | bytes 1048576

commit v3 on v2

--- a/solution.py
+++ b/solution.py
@@ -12,6 +12,7 @@
 LANES = 128
 LAYER_VMEM = 60 * 2**20
 SWAP_VMEM = 60 * 2**20
+SPREAD_VMEM = 52 * 2**20
 bf16 = jnp.bfloat16
 f32 = jnp.float32
 i32 = jnp.int32
@@ -50,9 +51,9 @@
 
 
 def fetch_kernel(shards, cap, ids_hbm, table_hbm, fetched_ref, slots_ref, asked_ref,
-                 table, mirror, requests, asks, answers, replies, columns, total,
+                 table, mirror, requests, asks, answers, replies, rows32, total, slots_smem, slots_sem,
                  ask_send, ask_recv, row_send, row_recv, far_send, far_recv, swap_send, swap_recv,
-                 tell_send, tell_recv, table_sem, ids_ref, ids_sem):
+                 table_sem, ids_ref, ids_sem):
     me, group = lax.axis_index("mem"), lax.axis_index("groups")
     groups = lax.axis_size("groups")
     half = shards // 2
@@ -104,12 +105,13 @@
         rank = jnp.sum(mine * ranks, axis=0, keepdims=True).astype(i32)
         slot = owner * cap + rank
         slots_ref[h:h + 1, :] = slot
-        columns[h] = as_column(slot)
         at_rank = one_hot(jnp.broadcast_to(rank, (wide, tokens)) == iota((wide, tokens), 0))
         high = (offset // 256).astype(f32)
         low = (offset % 256).astype(f32)
         parts = jnp.concatenate([mine * high, mine * low, mine], axis=0).astype(bf16)
         gathered = gathered + dot(parts, at_rank, NT)
+    slots_load = pltpu.make_async_copy(slots_ref, slots_smem, slots_sem)
+    slots_load.start()
     wanted = gathered[:shards] * 256.0 + gathered[shards:2 * shards]
     wanted = jnp.where(gathered[2 * shards:] > 0.5, wanted, -1.0).astype(i32)
     for block in range(shards):
@@ -137,9 +139,7 @@
         return carry
 
     lax.fori_loop(1, half, answer, 0)
-    asked_ref[0] = asks[0]
-    tell = remote(asks.at[1], asked_ref.at[1], tell_send, tell_recv, far)
-    tell.start()
+    asked_ref[...] = asks[...]
 
     to_far.wait_recv()
     if share < rows:
@@ -148,18 +148,9 @@
     replies[0, here] = rows_for(0, me, table)
 
     def unpack(side, peer):
-        block = replies[side, peer % half]
         base = ((home + side) % 2 * half + peer % half) * cap
-        for h in range(heads):
-            column = columns[h] - base
-            if cap % LANES == 0:
-                hot = jnp.concatenate(
-                    [one_hot(column == iota((tokens, LANES), 1) + start) for start in range(0, cap, LANES)], axis=1)
-            else:
-                hot = one_hot(column == iota((tokens, LANES), 1))[:, :cap]
-            total[:, h * LANES:(h + 1) * LANES] += dot(hot, block)
-
-    total[...] = jnp.zeros_like(total)
+        rows32[pl.ds(pl.multiple_of(base, 16), cap)] = replies[side, peer % half].astype(f32)
+
     unpack(0, me)
     if share < rows:
         remote(mirror.at[twin_at], mirror.at[twin_at], swap_send, swap_recv, twin).wait_recv()
@@ -182,7 +173,19 @@
             return carry
 
         lax.fori_loop(1, half, take, 0)
-    fetched_ref[...] = total[...].astype(bf16)
+    slots_load.wait()
+    group_of = 8
+
+    def pick(j, carry):
+        for i in range(group_of):
+            token = j * group_of + i
+            for h in range(heads):
+                total[h, pl.ds(token, 1), :] = rows32[pl.ds(jnp.clip(slots_smem[h, token], 0, shards * cap - 1), 1), :]
+        return carry
+
+    lax.fori_loop(0, tokens // group_of, pick, 0)
+    for h in range(heads):
+        fetched_ref[:, h * LANES:(h + 1) * LANES] = total[h].astype(bf16)
 
     def finish(step, carry):
         peer = partner(me, step, shards)
@@ -195,7 +198,6 @@
     to_far.wait_send()
     if share < rows:
         swap.wait_send()
-    tell.wait()
 
 
 def fetch(ids, table, shards, cap):
@@ -222,11 +224,11 @@
             pltpu.VMEM((2, half, 1, wide), i32),
             pltpu.VMEM((2, half, cap, width), bf16),
             pltpu.VMEM((2, half, cap, width), bf16),
-            pltpu.VMEM((heads, tokens, LANES), i32),
-            pltpu.VMEM((tokens, heads * width), f32),
+            pltpu.VMEM((shards * cap, width), f32),
+            pltpu.VMEM((heads, tokens, width), f32),
+            pltpu.SMEM((heads, tokens), i32), dma,
             dma((half,)), dma((half,)), dma((2, half)), dma((2, half)),
-            dma, dma, dma, dma, dma, dma,
-            dma, pltpu.VMEM((heads, tokens), i32), dma,
+            dma, dma, dma, dma, dma, pltpu.VMEM((heads, tokens), i32), dma,
         ],
         compiler_params=pltpu.CompilerParams(
             collective_id=0, has_side_effects=True, vmem_limit_bytes=SWAP_VMEM),
@@ -415,61 +417,72 @@
     )(lengths, fetched, hidden, cotangent, w_key, w_value, conv_weight)
 
 
-def spread_kernel(shards, cap, slots_ref, asked_ref, pieces_ref, grad_ref, outgoing, incoming, send, recv):
+def spread_kernel(shards, cap, slots_ref, asked_ref, pieces_ref, grad_ref,
+                  outgoing, incoming, partial, landed, send, recv, far_send, far_recv):
     me = lax.axis_index("mem")
+    half = shards // 2
+    home, here = me // half, me % half
+    far = {"mem": partner(me, half, shards)}
     heads, tokens = slots_ref.shape
     rows = grad_ref.shape[0]
 
-    def push(peer):
+    def push(side, peer, slot):
+        at = peer % half
         return pltpu.make_async_remote_copy(
-            src_ref=outgoing.at[peer], dst_ref=incoming.at[me],
-            send_sem=send.at[peer], recv_sem=recv.at[me], device_id={"mem": peer})
-
-    def pushed_by(peer):
-        return pltpu.make_async_remote_copy(
-            src_ref=outgoing.at[peer], dst_ref=incoming.at[peer],
-            send_sem=send.at[peer], recv_sem=recv.at[peer], device_id={"mem": peer})
-
-    def pack(peer):
+            src_ref=outgoing.at[side, at], dst_ref=incoming.at[side, slot],
+            send_sem=send.at[side, at], recv_sem=recv.at[side, slot], device_id={"mem": peer})
+
+    def pack(side, peer):
+        base = ((home + side) % 2 * half + peer % half) * cap
         packed = jnp.zeros((cap, LANES), f32)
         for h in range(heads):
-            row = slots_ref[h:h + 1, :] - peer * cap
+            row = slots_ref[h:h + 1, :] - base
             hot = one_hot(jnp.broadcast_to(row, (cap, tokens)) == iota((cap, tokens), 0))
             packed = packed + dot(hot, pieces_ref[:, h * LANES:(h + 1) * LANES])
         return packed.astype(bf16)
 
-    greet([{"mem": partner(me, step, shards)} for step in range(1, shards)])
-
-    def send_one(j, carry):
-        peer = partner(me, shards - j, shards)
-        outgoing[peer] = pack(peer)
-        push(peer).start()
-        return carry
-
-    lax.fori_loop(1, shards, send_one, 0)
-    incoming[me] = pack(me)
-
-    def add(peer):
-        half = shards // 2
-        row = asked_ref[(peer // half + me // half) % 2, peer % half][:, :cap]
+    def add(side, peer):
+        row = asked_ref[side, peer % half][:, :cap]
         hot = one_hot(jnp.broadcast_to(row, (rows, cap)) == iota((rows, cap), 0))
-        return dot(hot, incoming[peer])
-
-    grad_ref[...] = add(me)
-
-    def take(step, carry):
+        return dot(hot, incoming[side, peer % half])
+
+    greet([{"mem": partner(me, step, shards)} for step in range(1, half)] + [far])
+    to_far = pltpu.make_async_remote_copy(
+        src_ref=partial, dst_ref=landed, send_sem=far_send, recv_sem=far_recv, device_id=far)
+
+    for side in (1, 0):
+        def send_one(j, carry):
+            peer = partner(me, half - j, shards)
+            outgoing[side, peer % half] = pack(side, peer)
+            push(side, peer, here).start()
+            return carry
+
+        lax.fori_loop(1, half, send_one, 0)
+        incoming[side, here] = pack(side, me)
+        grad_ref[...] = add(side, me)
+
+        def take(step, carry):
+            peer = partner(me, step, shards)
+            push(side, peer, peer % half).wait_recv()
+            grad_ref[...] += add(side, peer)
+            return carry
+
+        lax.fori_loop(1, half, take, 0)
+        if side == 1:
+            partial[...] = grad_ref[...].astype(bf16)
+            to_far.start()
+
+    to_far.wait_recv()
+    grad_ref[...] += landed[...].astype(f32)
+
+    def finish(step, carry):
         peer = partner(me, step, shards)
-        pushed_by(peer).wait_recv()
-        grad_ref[...] += add(peer)
-        return carry
-
-    lax.fori_loop(1, shards, take, 0)
-
-    def finish(step, carry):
-        push(partner(me, step, shards)).wait_send()
-        return carry
-
-    lax.fori_loop(1, shards, finish, 0)
+        push(0, peer, here).wait_send()
+        push(1, peer, here).wait_send()
+        return carry
+
+    lax.fori_loop(1, half, finish, 0)
+    to_far.wait_send()
 
 
 def spread(slots, asked, pieces, rows, shards, cap):
@@ -480,13 +493,17 @@
         in_specs=[vmem] * 3,
         out_specs=vmem,
         scratch_shapes=[
-            pltpu.VMEM((shards, cap, LANES), bf16),
-            pltpu.VMEM((shards, cap, LANES), bf16),
-            pltpu.SemaphoreType.DMA((shards,)),
-            pltpu.SemaphoreType.DMA((shards,)),
+            pltpu.VMEM((2, shards // 2, cap, LANES), bf16),
+            pltpu.VMEM((2, shards // 2, cap, LANES), bf16),
+            pltpu.VMEM((rows, LANES), bf16),
+            pltpu.VMEM((rows, LANES), bf16),
+            pltpu.SemaphoreType.DMA((2, shards // 2)),
+            pltpu.SemaphoreType.DMA((2, shards // 2)),
+            pltpu.SemaphoreType.DMA,
+            pltpu.SemaphoreType.DMA,
         ],
         compiler_params=pltpu.CompilerParams(
-            collective_id=1, has_side_effects=True, vmem_limit_bytes=SWAP_VMEM),
+            collective_id=1, has_side_effects=True, vmem_limit_bytes=SPREAD_VMEM),
         name="spread",
     )(slots, asked, pieces)
 

time: 88.9 us -> 84.8 us (0.954)
  Pallas kernels: 86.2 us -> 82.1 us
    pallas_call x1, Pallas kernels: 32.6 us -> 26.1 us  [spread(): pl.pallas_call(functools.partial(spread_kernel, shards, cap), out_shape=j...]
    pallas_call x1, Pallas kernels: 30.9 us -> 33.4 us  [fetch(): pl.pallas_call(functools.partial(fetch_kernel, shards, cap), out_shape=(j...]
    unnamed x1 -> x7, local copies, waits for them, and re-layouts: 1.87 us -> 1.84 us
where the time goes in v3:
time: 84.8 us; the launch traced here: 84.6 us
  Pallas kernels  82.1 us (97%)
  local copies, waits for them, and re-layouts  1.84 us (2%)
    pallas_call x1, Pallas kernels, fetch(): pl.pallas_call(functools.partial(fetch_kernel, shards, cap), out_shape=(j...  33.4 us
    pallas_call x1, Pallas kernels, spread(): pl.pallas_call(functools.partial(spread_kernel, shards, cap), out_shape=j...  26.1 us
    pallas_call x1, Pallas kernels, layer(): pl.pallas_call(layer_kernel, out_shape=(jax.ShapeDtypeStruct((tokens, col...  22.6 us
    unnamed x7, local copies, waits for them, and re-layouts  1.84 us

profile of v3, /device:TPU:0, one launch (start us, length us, event | category | flops | bytes accessed | tf_op | source)
XLA Modules:
  0.0 84.6 jit_solution(13259246636360414824)
XLA Ops:
  0.6 33.4 %fetch.1 = (bf16[512,512]{1,0:T(8,128)(2,1)}, s32[4,512]{1,0:T(4,128)}, s32[2,8,1,256]{3,2,1,0:T(1,128)}) custom-call(s32[4,512]{1,0:T(4,128)} %bitcast.1, bf16[1024,128]{1,0:T(8,128)(2,1)} %table_hbm.1), custom_call_target="tpu_custom_call" | custom-call | tf_op jit(solution)/shard_map/fetch/pallas_call | solution.py:211
  34.0 0.0 copy-start.1
  34.0 0.0 copy-start.2
  34.0 22.6 %layer.1 = (bf16[512,2560]{1,0:T(8,128)(2,1)}, bf16[512,2560]{1,0:T(8,128)(2,1)}, bf16[512,512]{1,0:T(8,128)(2,1)}) custom-call(s32[1,4]{1,0:T(1,128)} %lengths_ref.1, bf16[512,512]{1,0:T(8,128)(2,1)} %get-tuple-element.9.fetched_ref, bf16[512,2560]{1,0:T(8,128)(2,1)} %hidden_hbm.1, bf16[512,2560]{1,0:T(8,128)(2,1)} %cotangent_hbm.1, ...), custom_call_target="tpu_custom_call" | custom-call | tf_op jit(solution)/shard_map/layer/pallas_call | solution.py:381
  56.7 0.0 copy-done.1
  56.7 0.0 copy-done.2
  56.7 0.0 copy-start
  56.7 1.0 %copy-done = bf16[512,512]{1,0:T(8,128)(2,1)S(1)} copy-done((bf16[512,512]{1,0:T(8,128)(2,1)S(1)}, bf16[512,512]{1,0:T(8,128)(2,1)}, u32[]{:S(2)}) %copy-start) | copy-done | bytes 524312
  57.7 26.1 %spread.1 = f32[1024,128]{1,0:T(8,128)S(1)} custom-call(s32[4,512]{1,0:T(4,128)S(1)} %copy-done.2, s32[2,8,1,256]{3,2,1,0:T(1,128)S(1)} %copy-done.1, bf16[512,512]{1,0:T(8,128)(2,1)S(1)} %copy-done), custom_call_target="tpu_custom_call" | custom-call | tf_op jit(solution)/shard_map/spread/pallas_call | solution.py:490
  83.8 0.8 copy.12
Async XLA Ops:
  34.0 22.6 %copy-start.1 = (s32[2,8,1,256]{3,2,1,0:T(1,128)S(1)}, s32[2,8,1,256]{3,2,1,0:T(1,128)}, u32[]{:S(2)}) copy-start(s32[2,8,1,256]{3,2,1,0:T(1,128)} %get-tuple-element.13.asked_ref) | copy-start | bytes 49156
  34.0 22.6 %copy-start.2 = (s32[4,512]{1,0:T(4,128)S(1)}, s32[4,512]{1,0:T(4,128)}, u32[]{:S(2)}) copy-start(s32[4,512]{1,0:T(4,128)} %get-tuple-element.12.slots_ref) | copy-start | bytes 24580
  56.7 1.0 %copy-start = (bf16[512,512]{1,0:T(8,128)(2,1)S(1)}, bf16[512,512]{1,0:T(8,128)(2,1)}, u32[]{:S(2)}) copy-start(bf16[512,512]{1,0:T(8,128)(2,1)} %get-tuple-element.14.pieces_ref) | copy-start | bytes 1572868
